TPU v7x, 32 devices: a whole 2x2x4 slice. The times are simulated.
32 devices in a mesh: dp: 8 (over y, x, core), inv: 4 (over z).
Axes of the slice: x: 2, y: 2, z: 4, core: 2. Of those that a mesh axis runs over, the one named last changes fastest.
Arguments:
- acts: bfloat16 [1024, 6144], P('dp', 'inv'), may hold values from -6 to 6
- grads_out: bfloat16 [1024, 24576], P('inv', 'dp'), may hold values from -0.119628906 to 0.119628906
- scale_exp: int32 [1024], replicated, may hold values from 0 to 3
- shard_tokens: int32 [8], replicated, may hold values from 1 to 128, 768 in all
Outputs:
- precond: bfloat16 [6144, 24576], P('inv', 'dp')
Inputs may be any that keep to these rules, and one draw needn't show every extreme that they name: `shard_tokens`: largest entry is exactly 128; entries sum to 768.
All inputs are finite; a program needn't handle non-finite values.
Results may differ from a plain program's by a relative error of at most 0.0015.
Values may be sent and summed in bfloat16 or wider, within the bound.
A program may use at most 64 MiB of HBM per device.

v0:
```python
import functools

import jax
import jax.numpy as jnp
from jax import lax
from jax.experimental import pallas as pl
from jax.experimental.pallas import tpu as pltpu
from jax.sharding import PartitionSpec as P

BLK = 128
ITERS = 8
TOK_DEV = 128
WIDTH = 256
AHEAD = 4
DAMPING = 0.001
MESH = pl.DeviceIdType.MESH
f32, bf16 = jnp.float32, jnp.bfloat16


def dot(a, b, dims=((1,), (0,))):
    return lax.dot_general(a, b, (dims, ((), ())), preferred_element_type=f32)


def split(x):
    hi = x.astype(bf16)
    return hi, (x - hi.astype(f32)).astype(bf16)


def pairs(hi, lo):
    row = jnp.concatenate([hi, lo], axis=1)
    return row, jnp.concatenate([row, row], axis=0)


def halves(r):
    return r[:, :BLK] + r[:, BLK:]


def newton(covs):
    i = lax.broadcasted_iota(jnp.int32, (BLK, BLK), 0)
    j = lax.broadcasted_iota(jnp.int32, (BLK, BLK), 1)
    diag = i == j
    ts, xs, invs = [], [], []
    for c in covs:
        tr = jnp.sum(jnp.where(diag, c, 0.0), keepdims=True)
        m = c + jnp.where(diag, DAMPING * (tr / BLK), 0.0)
        inv = 1.0 / jnp.sum(jnp.where(diag, m, 0.0), keepdims=True)
        t = m * inv
        ts.append(t)
        xs.append(jnp.where(diag, 2.0, 0.0) - t)
        invs.append(inv)
    for step in range(ITERS):
        for b in range(len(covs)):
            t, x = ts[b], xs[b]
            t_row, t_mat = pairs(*split(t))
            if step == 0:
                ts[b] = 2.0 * t - halves(dot(t_row, t_mat))
                continue
            x_row = jnp.concatenate(split(x), axis=1)
            if step == ITERS - 1:
                xs[b] = 2.0 * x - halves(dot(x_row, t_mat))
                continue
            r = halves(dot(jnp.concatenate([t_row, x_row], axis=0), t_mat))
            ts[b] = 2.0 * t - r[:BLK]
            xs[b] = 2.0 * x - r[BLK:]
    return [x * inv for x, inv in zip(xs, invs)]


def kernel(n_dp, n_inv, cap, acts_t, grads, pos_col, pos_row, w_row, count, out,
           acts_all, place, pa, fl, fr, own, stage,
           a_send, a_recv, l_send, l_recv, r_send, r_recv, o_sem):
    dp = lax.axis_index("dp")
    z = lax.axis_index("inv")
    units = acts_t.shape[0]
    tp = grads.shape[0]
    chunks, live, width = own.shape
    tokens = pos_col.shape[0]

    barrier = pltpu.get_barrier_semaphore()

    def greet(d, _):
        pl.semaphore_signal(barrier, inc=1, device_id={"dp": lax.rem(dp + d, n_dp)}, device_id_type=MESH)
        return 0

    lax.fori_loop(1, n_dp, greet, 0)

    @pl.when(z > 0)
    def _():
        pl.semaphore_signal(barrier, inc=1, device_id={"inv": z - 1}, device_id_type=MESH)

    @pl.when(z < n_inv - 1)
    def _():
        pl.semaphore_signal(barrier, inc=1, device_id={"inv": z + 1}, device_id_type=MESH)

    at_end = (z == 0) | (z == n_inv - 1)

    @pl.when(at_end)
    def _():
        pl.semaphore_wait(barrier, n_dp)

    @pl.when(jnp.logical_not(at_end))
    def _():
        pl.semaphore_wait(barrier, n_dp + 1)

    def acts_copy(owner, peer):
        cols = pl.ds(pl.multiple_of(owner * TOK_DEV, TOK_DEV), TOK_DEV)
        return pltpu.make_async_remote_copy(
            src_ref=acts_t, dst_ref=acts_all.at[:, cols], send_sem=a_send.at[peer], recv_sem=a_recv.at[owner],
            device_id={"dp": peer}, device_id_type=MESH)

    def send_acts(d, _):
        acts_copy(dp, lax.rem(dp + d, n_dp)).start()
        return 0

    lax.fori_loop(1, n_dp, send_acts, 0)

    def wait_acts(d, _):
        peer = lax.rem(dp + d, n_dp)
        acts_copy(peer, peer).wait_recv()
        return 0

    def wait_acts_sent(d, _):
        acts_copy(dp, lax.rem(dp + d, n_dp)).wait_send()
        return 0

    hops = min(-(-cap // tp), n_inv - 1)
    left_rows = []
    right_rows = []
    for k in range(hops):
        hi = live - k * tp
        lo = max(live - cap, hi - tp)
        left_rows.append((lo, hi - lo))
        right_rows.append((k * tp, min(cap, (k + 1) * tp) - k * tp))

    def left_copy(c, k):
        lo, size = left_rows[k]
        part = fr.at[c, pl.ds(lo, size), :]
        return pltpu.make_async_remote_copy(
            src_ref=part, dst_ref=part, send_sem=l_send.at[k, c], recv_sem=l_recv.at[k, c],
            device_id={"inv": lax.max(z - 1, 0)}, device_id_type=MESH)

    def right_copy(c, k):
        lo, size = right_rows[k]
        part = fl.at[c, pl.ds(lo, size), :]
        return pltpu.make_async_remote_copy(
            src_ref=part, dst_ref=part, send_sem=r_send.at[k, c], recv_sem=r_recv.at[k, c],
            device_id={"inv": lax.min(z + 1, n_inv - 1)}, device_id_type=MESH)

    def leftward(c):
        if cap < live:
            fr[c, :live - cap, :] = own[c, :live - cap, :]
        for k in range(hops):
            lo, size = left_rows[k]
            rows = pl.ds(lo, size)

            @pl.when(z < n_inv - 1 - k)
            def _():
                left_copy(c, k).wait_recv()
                fr[c, rows, :] = fr[c, rows, :] + own[c, rows, :]

            @pl.when(z >= n_inv - 1 - k)
            def _():
                fr[c, rows, :] = own[c, rows, :]

            @pl.when((z > 0) & (z < n_inv - k))
            def _():
                left_copy(c, k).start()

    def rightward(c):
        if cap < live:
            fl[c, cap:, :] = own[c, cap:, :]
        for k in range(hops):
            lo, size = right_rows[k]
            rows = pl.ds(lo, size)

            @pl.when(z > k)
            def _():
                right_copy(c, k).wait_recv()
                fl[c, rows, :] = fl[c, rows, :] + own[c, rows, :]

            @pl.when(z <= k)
            def _():
                fl[c, rows, :] = own[c, rows, :]

            @pl.when((z < n_inv - 1) & (z >= k))
            def _():
                right_copy(c, k).start()

    slot = lax.broadcasted_iota(jnp.int32, (live, tp), 0)
    place_own = jnp.where(slot == pos_row[...], w_row[...], 0.0).astype(bf16)

    def relay(c, _):
        cols = pl.ds(pl.multiple_of(c * width, width), width)
        own[c] = dot(place_own, grads[:, cols]).astype(bf16)

        @pl.when(z >= n_inv // 2)
        def _():
            leftward(c)

        rightward(c)

        @pl.when(z < n_inv // 2)
        def _():
            leftward(c)

        both = fr[c].astype(f32) + fl[c].astype(f32)
        own[c] = (both - own[c].astype(f32)).astype(bf16)
        return 0

    ahead = min(AHEAD, chunks)
    lax.fori_loop(0, ahead, relay, 0)

    def fill(s, _):
        rows = pl.ds(pl.multiple_of(s * TOK_DEV, TOK_DEV), TOK_DEV)
        spot = lax.broadcasted_iota(jnp.int32, (TOK_DEV, live), 1)
        place[rows, :] = jnp.where(spot == pos_col[rows, :], 1.0, 0.0).astype(bf16)
        return 0

    lax.fori_loop(0, tokens // TOK_DEV, fill, 0)
    acts_all[:, pl.ds(pl.multiple_of(dp * TOK_DEV, TOK_DEV), TOK_DEV)] = acts_t[...]
    lax.fori_loop(1, n_dp, wait_acts, 0)

    a_blocks = units // BLK
    group = max(g for g in (1, 2, 3, 4) if a_blocks % g == 0)

    def input_side(g, _):
        rows = [pl.ds(pl.multiple_of((g * group + i) * BLK, BLK), BLK) for i in range(group)]
        masked = [dot(acts_all[r, :], place[...]).astype(bf16) for r in rows]
        covs = [dot(m, m, ((1,), (1,))) for m in masked]
        for r, m, x in zip(rows, masked, newton(covs)):
            x_row = jnp.concatenate(split(x * count[...]), axis=1)
            hi, lo = split(dot(x_row, jnp.concatenate([m, m], axis=0)))
            pa[r, :live] = hi
            pa[r, live:2 * live] = lo
            pa[r, 2 * live:] = hi
        return 0

    lax.fori_loop(0, a_blocks // group, input_side, 0)

    step_rows = 512 if units % 512 == 0 else units

    def out_copy(c):
        cols = pl.ds(pl.multiple_of(c * width, width), width)
        return pltpu.make_async_copy(stage.at[c], out.at[:, cols], o_sem.at[c])

    def finish(c):
        parts = [own[c, :, i * BLK:(i + 1) * BLK] for i in range(width // BLK)]
        covs = [dot(s, s, ((0,), (0,))) for s in parts]
        his, los = [], []
        for s, x in zip(parts, newton(covs)):
            hi, lo = split(halves(dot(s, jnp.concatenate(split(x), axis=1))))
            his.append(hi)
            los.append(lo)
        hi = jnp.concatenate(his, axis=1)
        q = jnp.concatenate([hi, hi, jnp.concatenate(los, axis=1)], axis=0)

        def rows_step(m, _):
            rows = pl.ds(pl.multiple_of(m * step_rows, step_rows), step_rows)
            stage[c, rows, :] = dot(pa[rows, :], q).astype(bf16)
            return 0

        lax.fori_loop(0, units // step_rows, rows_step, 0)
        out_copy(c).start()

    def main(c, _):
        @pl.when(c + ahead < chunks)
        def _():
            relay(c + ahead, 0)

        finish(c)
        return 0

    lax.fori_loop(0, chunks, main, 0)

    lax.fori_loop(1, n_dp, wait_acts_sent, 0)

    def drain(c, _):
        out_copy(c).wait()
        for k in range(hops):
            @pl.when((z > 0) & (z < n_inv - k))
            def _():
                left_copy(c, k).wait_send()

            @pl.when((z < n_inv - 1) & (z >= k))
            def _():
                right_copy(c, k).wait_send()
        return 0

    lax.fori_loop(0, chunks, drain, 0)


def call(n_dp, n_inv, cap, collective_id, acts_t, grads, pos_col, pos_row, w_row, count):
    units, tp, cols = acts_t.shape[0], grads.shape[0], grads.shape[1]
    tokens = pos_col.shape[0]
    live = tokens * 3 // 4
    chunks = cols // WIDTH
    hops = min(-(-cap // tp), n_inv - 1)
    vmem = pl.BlockSpec(memory_space=pltpu.VMEM)
    return pl.pallas_call(
        functools.partial(kernel, n_dp, n_inv, cap),
        out_shape=jax.ShapeDtypeStruct((units, cols), bf16),
        in_specs=[vmem] * 6,
        out_specs=pl.BlockSpec(memory_space=pl.ANY),
        scratch_shapes=[
            pltpu.VMEM((units, tokens), bf16),
            pltpu.VMEM((tokens, live), bf16),
            pltpu.VMEM((units, 3 * live), bf16),
            pltpu.VMEM((chunks, live, WIDTH), bf16),
            pltpu.VMEM((chunks, live, WIDTH), bf16),
            pltpu.VMEM((chunks, live, WIDTH), bf16),
            pltpu.VMEM((chunks, units, WIDTH), bf16),
            pltpu.SemaphoreType.DMA((n_dp,)),
            pltpu.SemaphoreType.DMA((n_dp,)),
            pltpu.SemaphoreType.DMA((hops, chunks)),
            pltpu.SemaphoreType.DMA((hops, chunks)),
            pltpu.SemaphoreType.DMA((hops, chunks)),
            pltpu.SemaphoreType.DMA((hops, chunks)),
            pltpu.SemaphoreType.DMA((chunks,)),
        ],
        compiler_params=pltpu.CompilerParams(
            collective_id=collective_id, has_side_effects=True, vmem_limit_bytes=60 * 2**20),
        cost_estimate=pl.CostEstimate(
            flops=6 * units * live * cols, bytes_accessed=4 * units * cols, transcendentals=0),
    )(acts_t, grads, pos_col, pos_row, w_row, count)


def local(n_dp, n_inv, acts, grads_out, scale_exp, shard_tokens):
    tp = grads_out.shape[0]
    tokens = acts.shape[0] * n_dp
    ids = jnp.arange(tokens, dtype=jnp.int32)
    in_shard = ids % TOK_DEV
    limit = jnp.repeat(shard_tokens, TOK_DEV)
    first = jnp.repeat(jnp.cumsum(shard_tokens) - shard_tokens, TOK_DEV)
    pos = jnp.where(in_shard < limit, first + in_shard, -1).astype(jnp.int32)
    weight = jnp.exp2(-scale_exp.astype(f32))
    start = lax.axis_index("inv") * tp
    pos_row = lax.dynamic_slice_in_dim(pos, start, tp)[None, :]
    w_row = lax.dynamic_slice_in_dim(weight, start, tp)[None, :]
    count = jnp.sum(shard_tokens).astype(f32).reshape(1, 1)
    live = tokens * 3 // 4
    return call(n_dp, n_inv, live, 0, acts.T, grads_out, pos[:, None], pos_row, w_row, count)


def solution(mesh):
    placed = (P("dp", "inv"), P("inv", "dp"), P(), P())
    return jax.shard_map(
        functools.partial(local, mesh.shape["dp"], mesh.shape["inv"]),
        mesh=mesh, in_specs=placed, out_specs=P("inv", "dp"), check_vma=False)
```

profile of v0, /device:TPU:24, one launch (start us, length us, event | category | flops | bytes accessed | tf_op | source)
XLA Modules:
  0.0 295.6 jit_solution(7108160169669777803)
XLA Ops:
  0.0 0.8 reduce-window.9
  0.8 1.3 fusion.8
  2.8 0.7 fusion.4
  3.5 0.6 dynamic_slice.6
  4.1 0.1 broadcast_in_dim.20
  4.2 0.7 multiply_exponential_fusion
  4.9 0.6 dynamic_slice.7
  5.5 0.7 broadcast_in_dim.19
  6.2 1.9 copy.6
  8.1 0.2 copy.7
  8.4 0.2 copy.8
  8.6 0.9 add_select_fusion.1.pos_col
  9.5 277.8 %shard_map.46 = bf16[1536,3072]{1,0:T(8,128)(2,1)} custom-call(bf16[1536,128]{1,0:T(8,128)(2,1)} %bitcast.17, bf16[256,3072]{1,0:T(8,128)(2,1)} %grads.1, s32[1024,1]{1,0:T(8,128)} %add_select_fusion.1.pos_col, s32[1,256]{1,0:T(1,128)} %bitcast.21, f32[1,256]{1,0:T(1,128)} %bitcast.22, f32[1,1]{1,0:T(1,128)} %bitcast.9.count), custom_call_target="tpu_custom_call" | custom-call | flops 21743271936 | bytes 18874368 | tf_op jit(solution)/shard_map/pallas_call | solution.py:298
  287.3 8.3 %copy.10 = bf16[1536,3072]{1,0:T(8,128)(2,1)} copy(bf16[1536,3072]{1,0:T(8,128)(2,1)} %shard_map.46) | data formatting | bytes 18874368
where the time goes:
time: 296 us
  Pallas kernels  278 us (94%)
  local copies, waits for them, and re-layouts  12.6 us (4%)
  other arithmetic  4.43 us (1%)
    pallas_call x1, Pallas kernels, call(): pl.pallas_call(functools.partial(kernel, n_dp, n_inv, cap), out_shape=jax...  278 us
    unnamed x2, local copies, waits for them, and re-layouts  10.2 us

commit v1 on v0

--- a/solution.py
+++ b/solution.py
@@ -11,7 +11,6 @@
 ITERS = 8
 TOK_DEV = 128
 WIDTH = 256
-AHEAD = 4
 DAMPING = 0.001
 MESH = pl.DeviceIdType.MESH
 f32, bf16 = jnp.float32, jnp.bfloat16
@@ -66,7 +65,7 @@
 
 
 def kernel(n_dp, n_inv, cap, acts_t, grads, pos_col, pos_row, w_row, count, out,
-           acts_all, place, pa, fl, fr, own, stage,
+           acts_all, place, pa, fl, fr, own, q, stage,
            a_send, a_recv, l_send, l_recv, r_send, r_recv, o_sem):
     dp = lax.axis_index("dp")
     z = lax.axis_index("inv")
@@ -196,35 +195,82 @@
         def _():
             leftward(c)
 
-        rightward(c)
-
-        @pl.when(z < n_inv // 2)
+        @pl.when(z < n_inv - 1)
+        def _():
+            rightward(c)
+
+        @pl.when((z > 0) & (z < n_inv // 2))
         def _():
             leftward(c)
+
+        return 0
+
+    def merge(c):
+        @pl.when(z == 0)
+        def _():
+            leftward(c)
+
+        @pl.when(z == n_inv - 1)
+        def _():
+            rightward(c)
 
         both = fr[c].astype(f32) + fl[c].astype(f32)
         own[c] = (both - own[c].astype(f32)).astype(bf16)
-        return 0
-
-    ahead = min(AHEAD, chunks)
-    lax.fori_loop(0, ahead, relay, 0)
-
-    def fill(s, _):
-        rows = pl.ds(pl.multiple_of(s * TOK_DEV, TOK_DEV), TOK_DEV)
-        spot = lax.broadcasted_iota(jnp.int32, (TOK_DEV, live), 1)
-        place[rows, :] = jnp.where(spot == pos_col[rows, :], 1.0, 0.0).astype(bf16)
-        return 0
-
-    lax.fori_loop(0, tokens // TOK_DEV, fill, 0)
+
+    pair = 2 if chunks % 2 == 0 else 1
+    early = min(2, chunks // pair)
+
+    def output_side(p, _):
+        spots = [(p * pair + i // (width // BLK), i % (width // BLK)) for i in range(pair * width // BLK)]
+        for i in range(pair):
+            merge(p * pair + i)
+        parts = [own[c, :, j * BLK:(j + 1) * BLK] for c, j in spots]
+        covs = [dot(s, s, ((0,), (0,))) for s in parts]
+        for (c, j), s, x in zip(spots, parts, newton(covs)):
+            hi, lo = split(halves(dot(s, jnp.concatenate(split(x), axis=1))))
+            cols = slice(j * BLK, (j + 1) * BLK)
+            q[c, :live, cols] = hi
+            q[c, live:2 * live, cols] = hi
+            q[c, 2 * live:, cols] = lo
+        return 0
+
+    done = 0
+    for p, more in ((0, 4), (1, 3)):
+        if p < early:
+            lax.fori_loop(done, min(done + more, chunks), relay, 0)
+            done = min(done + more, chunks)
+            output_side(p, 0)
+    lax.fori_loop(done, min(done + 2, chunks), relay, 0)
+    done = min(done + 2, chunks)
+
     acts_all[:, pl.ds(pl.multiple_of(dp * TOK_DEV, TOK_DEV), TOK_DEV)] = acts_t[...]
     lax.fori_loop(1, n_dp, wait_acts, 0)
+    step_rows = 512 if units % 512 == 0 else units
+    piece = place.shape[0]
+    for at in range(0, tokens, piece):
+        def fill(s, _):
+            rows = pl.ds(pl.multiple_of(s * TOK_DEV, TOK_DEV), TOK_DEV)
+            ids = pl.ds(pl.multiple_of(at + s * TOK_DEV, TOK_DEV), TOK_DEV)
+            spot = lax.broadcasted_iota(jnp.int32, (TOK_DEV, live), 1)
+            place[rows, :] = jnp.where(spot == pos_col[ids, :], 1.0, 0.0).astype(bf16)
+            return 0
+
+        lax.fori_loop(0, piece // TOK_DEV, fill, 0)
+
+        def put(m, _):
+            rows = pl.ds(pl.multiple_of(m * step_rows, step_rows), step_rows)
+            r = dot(acts_all[rows, at:at + piece], place[...]).astype(bf16)
+            pa[rows, 2 * live:] = r if at == 0 else pa[rows, 2 * live:] + r
+            return 0
+
+        lax.fori_loop(0, units // step_rows, put, 0)
 
     a_blocks = units // BLK
     group = max(g for g in (1, 2, 3, 4) if a_blocks % g == 0)
 
     def input_side(g, _):
         rows = [pl.ds(pl.multiple_of((g * group + i) * BLK, BLK), BLK) for i in range(group)]
-        masked = [dot(acts_all[r, :], place[...]).astype(bf16) for r in rows]
+        masked = [pa[r, 2 * live:] for r in rows]
         covs = [dot(m, m, ((1,), (1,))) for m in masked]
         for r, m, x in zip(rows, masked, newton(covs)):
             x_row = jnp.concatenate(split(x * count[...]), axis=1)
@@ -232,44 +278,38 @@
             pa[r, :live] = hi
             pa[r, live:2 * live] = lo
             pa[r, 2 * live:] = hi
+
+        @pl.when(done + g < chunks)
+        def _():
+            relay(done + g, 0)
+
         return 0
 
     lax.fori_loop(0, a_blocks // group, input_side, 0)
-
-    step_rows = 512 if units % 512 == 0 else units
+    lax.fori_loop(min(done + a_blocks // group, chunks), chunks, relay, 0)
 
     def out_copy(c):
         cols = pl.ds(pl.multiple_of(c * width, width), width)
         return pltpu.make_async_copy(stage.at[c], out.at[:, cols], o_sem.at[c])
 
-    def finish(c):
-        parts = [own[c, :, i * BLK:(i + 1) * BLK] for i in range(width // BLK)]
-        covs = [dot(s, s, ((0,), (0,))) for s in parts]
-        his, los = [], []
-        for s, x in zip(parts, newton(covs)):
-            hi, lo = split(halves(dot(s, jnp.concatenate(split(x), axis=1))))
-            his.append(hi)
-            los.append(lo)
-        hi = jnp.concatenate(his, axis=1)
-        q = jnp.concatenate([hi, hi, jnp.concatenate(los, axis=1)], axis=0)
-
+    def finish(c, _):
         def rows_step(m, _):
             rows = pl.ds(pl.multiple_of(m * step_rows, step_rows), step_rows)
-            stage[c, rows, :] = dot(pa[rows, :], q).astype(bf16)
+            stage[c, rows, :] = dot(pa[rows, :], q[c]).astype(bf16)
             return 0
 
         lax.fori_loop(0, units // step_rows, rows_step, 0)
         out_copy(c).start()
-
-    def main(c, _):
-        @pl.when(c + ahead < chunks)
-        def _():
-            relay(c + ahead, 0)
-
-        finish(c)
-        return 0
-
-    lax.fori_loop(0, chunks, main, 0)
+        return 0
+
+    lax.fori_loop(0, early * pair, finish, 0)
+
+    def main(p, _):
+        output_side(p, 0)
+        lax.fori_loop(p * pair, p * pair + pair, finish, 0)
+        return 0
+
+    lax.fori_loop(early, chunks // pair, main, 0)
 
     lax.fori_loop(1, n_dp, wait_acts_sent, 0)
 
@@ -302,11 +342,12 @@
         out_specs=pl.BlockSpec(memory_space=pl.ANY),
         scratch_shapes=[
             pltpu.VMEM((units, tokens), bf16),
-            pltpu.VMEM((tokens, live), bf16),
+            pltpu.VMEM((min(tokens, 1024), live), bf16),
             pltpu.VMEM((units, 3 * live), bf16),
             pltpu.VMEM((chunks, live, WIDTH), bf16),
             pltpu.VMEM((chunks, live, WIDTH), bf16),
             pltpu.VMEM((chunks, live, WIDTH), bf16),
+            pltpu.VMEM((chunks, 3 * live, WIDTH), bf16),
             pltpu.VMEM((chunks, units, WIDTH), bf16),
             pltpu.SemaphoreType.DMA((n_dp,)),
             pltpu.SemaphoreType.DMA((n_dp,)),

time: 296 us -> 172 us (0.58)
  the two profiles are of different devices: /device:TPU:24 before, /device:TPU:20 now
where the time goes in v1:
time: 172 us
  Pallas kernels  154 us (90%)
  local copies, waits for them, and re-layouts  12.6 us (7%)
  other arithmetic  4.43 us (3%)
    pallas_call x1, Pallas kernels, call(): pl.pallas_call(functools.partial(kernel, n_dp, n_inv, cap), out_shape=jax...  154 us
    unnamed x2, local copies, waits for them, and re-layouts  10.2 us

profile of v1, /device:TPU:20, one launch (start us, length us, event | category | flops | bytes accessed | tf_op | source)
XLA Modules:
  0.0 172.2 jit_solution(10964485661809359196)
XLA Ops:
  0.0 0.8 reduce-window.9
  0.8 1.3 fusion.8
  2.8 0.7 fusion.4
  3.5 0.6 dynamic_slice.6
  4.1 0.1 broadcast_in_dim.20
  4.2 0.7 multiply_exponential_fusion
  4.9 0.6 dynamic_slice.7
  5.5 0.7 broadcast_in_dim.19
  6.2 1.9 %copy.6 = bf16[128,1536]{0,1:T(8,128)(2,1)} copy(bf16[128,1536]{1,0:T(8,128)(2,1)} %param.4) | data formatting | bytes 786432 | tf_op args[0]
  8.1 0.2 copy.7
  8.4 0.2 copy.8
  8.6 0.9 add_select_fusion.1.pos_col
  9.5 154.4 %shard_map.46 = bf16[1536,3072]{1,0:T(8,128)(2,1)} custom-call(bf16[1536,128]{1,0:T(8,128)(2,1)} %bitcast.17, bf16[256,3072]{1,0:T(8,128)(2,1)} %grads.1, s32[1024,1]{1,0:T(8,128)} %add_select_fusion.1.pos_col, s32[1,256]{1,0:T(1,128)} %bitcast.21, f32[1,256]{1,0:T(1,128)} %bitcast.22, f32[1,1]{1,0:T(1,128)} %bitcast.9.count), custom_call_target="tpu_custom_call" | custom-call | flops 21743271936 | bytes 18874368 | tf_op jit(solution)/shard_map/pallas_call | solution.py:338
  163.9 8.3 %copy.10 = bf16[1536,3072]{1,0:T(8,128)(2,1)} copy(bf16[1536,3072]{1,0:T(8,128)(2,1)} %shard_map.46) | data formatting | bytes 18874368

commit v2 on v1

--- a/solution.py
+++ b/solution.py
@@ -64,7 +64,7 @@
     return [x * inv for x, inv in zip(xs, invs)]
 
 
-def kernel(n_dp, n_inv, cap, acts_t, grads, pos_col, pos_row, w_row, count, out,
+def kernel(n_dp, n_inv, cap, acts_t, grads, pos_col, pos_row, exps, count, out,
            acts_all, place, pa, fl, fr, own, q, stage,
            a_send, a_recv, l_send, l_recv, r_send, r_recv, o_sem):
     dp = lax.axis_index("dp")
@@ -185,9 +185,12 @@
                 right_copy(c, k).start()
 
     slot = lax.broadcasted_iota(jnp.int32, (live, tp), 0)
-    place_own = jnp.where(slot == pos_row[...], w_row[...], 0.0).astype(bf16)
-
-    def relay(c, _):
+    mine = pl.ds(pl.multiple_of(z * tp, TOK_DEV), tp)
+    e = exps[:, mine]
+    weight = jnp.where(e == 0, 1.0, jnp.where(e == 1, 0.5, jnp.where(e == 2, 0.25, 0.125)))
+    place_own = jnp.where(slot == pos_row[:, mine], weight, 0.0).astype(bf16)
+
+    def near(c, _):
         cols = pl.ds(pl.multiple_of(c * width, width), width)
         own[c] = dot(place_own, grads[:, cols]).astype(bf16)
 
@@ -195,15 +198,32 @@
         def _():
             leftward(c)
 
-        @pl.when(z < n_inv - 1)
+        @pl.when(z < n_inv // 2)
         def _():
             rightward(c)
 
-        @pl.when((z > 0) & (z < n_inv // 2))
+        return 0
+
+    def far(c, _):
+        @pl.when((z >= n_inv // 2) & (z < n_inv - 1))
+        def _():
+            rightward(c)
+
+        @pl.when((z < n_inv // 2) & (z > 0))
         def _():
             leftward(c)
 
         return 0
+
+    at = {"near": 0, "far": 0}
+
+    def advance(nears, fars):
+        to = min(at["near"] + nears, chunks)
+        lax.fori_loop(at["near"], to, near, 0)
+        at["near"] = to
+        to = min(at["far"] + fars, to)
+        lax.fori_loop(at["far"], to, far, 0)
+        at["far"] = to
 
     def merge(c):
         @pl.when(z == 0)
@@ -234,23 +254,22 @@
             q[c, 2 * live:, cols] = lo
         return 0
 
-    done = 0
-    for p, more in ((0, 4), (1, 3)):
+    advance(4, 2)
+    for p, (nears, fars) in enumerate(((2, 0), (2, 3))):
         if p < early:
-            lax.fori_loop(done, min(done + more, chunks), relay, 0)
-            done = min(done + more, chunks)
+            advance(nears, max(fars, (p + 1) * pair - at["far"]))
             output_side(p, 0)
-    lax.fori_loop(done, min(done + 2, chunks), relay, 0)
-    done = min(done + 2, chunks)
+    advance(2, 3)
+    near_done, far_done = at["near"], at["far"]
 
     acts_all[:, pl.ds(pl.multiple_of(dp * TOK_DEV, TOK_DEV), TOK_DEV)] = acts_t[...]
     lax.fori_loop(1, n_dp, wait_acts, 0)
     step_rows = 512 if units % 512 == 0 else units
     piece = place.shape[0]
-    for at in range(0, tokens, piece):
+    for base in range(0, tokens, piece):
         def fill(s, _):
             rows = pl.ds(pl.multiple_of(s * TOK_DEV, TOK_DEV), TOK_DEV)
-            ids = pl.ds(pl.multiple_of(at + s * TOK_DEV, TOK_DEV), TOK_DEV)
+            ids = pl.ds(pl.multiple_of(base + s * TOK_DEV, TOK_DEV), TOK_DEV)
             spot = lax.broadcasted_iota(jnp.int32, (TOK_DEV, live), 1)
             place[rows, :] = jnp.where(spot == pos_col[ids, :], 1.0, 0.0).astype(bf16)
             return 0
@@ -259,8 +278,8 @@
 
         def put(m, _):
             rows = pl.ds(pl.multiple_of(m * step_rows, step_rows), step_rows)
-            r = dot(acts_all[rows, at:at + piece], place[...]).astype(bf16)
-            pa[rows, 2 * live:] = r if at == 0 else pa[rows, 2 * live:] + r
+            r = dot(acts_all[rows, base:base + piece], place[...]).astype(bf16)
+            pa[rows, 2 * live:] = r if base == 0 else pa[rows, 2 * live:] + r
             return 0
 
         lax.fori_loop(0, units // step_rows, put, 0)
@@ -279,14 +298,20 @@
             pa[r, live:2 * live] = lo
             pa[r, 2 * live:] = hi
 
-        @pl.when(done + g < chunks)
-        def _():
-            relay(done + g, 0)
-
-        return 0
-
-    lax.fori_loop(0, a_blocks // group, input_side, 0)
-    lax.fori_loop(min(done + a_blocks // group, chunks), chunks, relay, 0)
+        @pl.when(near_done + g < chunks)
+        def _():
+            near(near_done + g, 0)
+
+        @pl.when(far_done + g < chunks)
+        def _():
+            far(far_done + g, 0)
+
+        return 0
+
+    groups = a_blocks // group
+    lax.fori_loop(0, groups, input_side, 0)
+    lax.fori_loop(min(near_done + groups, chunks), chunks, near, 0)
+    lax.fori_loop(min(far_done + groups, chunks), chunks, far, 0)
 
     def out_copy(c):
         cols = pl.ds(pl.multiple_of(c * width, width), width)
@@ -328,7 +353,7 @@
     lax.fori_loop(0, chunks, drain, 0)
 
 
-def call(n_dp, n_inv, cap, collective_id, acts_t, grads, pos_col, pos_row, w_row, count):
+def call(n_dp, n_inv, cap, collective_id, acts_t, grads, pos_col, pos_row, exps, count):
     units, tp, cols = acts_t.shape[0], grads.shape[0], grads.shape[1]
     tokens = pos_col.shape[0]
     live = tokens * 3 // 4
@@ -361,24 +386,20 @@
             collective_id=collective_id, has_side_effects=True, vmem_limit_bytes=60 * 2**20),
         cost_estimate=pl.CostEstimate(
             flops=6 * units * live * cols, bytes_accessed=4 * units * cols, transcendentals=0),
-    )(acts_t, grads, pos_col, pos_row, w_row, count)
+    )(acts_t, grads, pos_col, pos_row, exps, count)
 
 
 def local(n_dp, n_inv, acts, grads_out, scale_exp, shard_tokens):
-    tp = grads_out.shape[0]
     tokens = acts.shape[0] * n_dp
-    ids = jnp.arange(tokens, dtype=jnp.int32)
-    in_shard = ids % TOK_DEV
-    limit = jnp.repeat(shard_tokens, TOK_DEV)
-    first = jnp.repeat(jnp.cumsum(shard_tokens) - shard_tokens, TOK_DEV)
-    pos = jnp.where(in_shard < limit, first + in_shard, -1).astype(jnp.int32)
-    weight = jnp.exp2(-scale_exp.astype(f32))
-    start = lax.axis_index("inv") * tp
-    pos_row = lax.dynamic_slice_in_dim(pos, start, tp)[None, :]
-    w_row = lax.dynamic_slice_in_dim(weight, start, tp)[None, :]
+    shards = tokens // TOK_DEV
+    order = jnp.arange(shards)
+    first = jnp.sum(jnp.where(order[None, :] < order[:, None], shard_tokens[None, :], 0), axis=1)
+    spot = jnp.arange(TOK_DEV, dtype=jnp.int32)[None, :]
+    pos = jnp.where(spot < shard_tokens[:, None], first[:, None] + spot, -1).astype(jnp.int32)
     count = jnp.sum(shard_tokens).astype(f32).reshape(1, 1)
     live = tokens * 3 // 4
-    return call(n_dp, n_inv, live, 0, acts.T, grads_out, pos[:, None], pos_row, w_row, count)
+    return call(n_dp, n_inv, live, 0, acts.T, grads_out, pos.reshape(tokens, 1), pos.reshape(1, tokens),
+                scale_exp.reshape(1, tokens), count)
 
 
 def solution(mesh):

time: 172 us -> 156 us (0.907)
  the two profiles are of different devices: /device:TPU:20 before, /device:TPU:24 now
where the time goes in v2:
time: 156 us; the launch traced here: 154 us
  Pallas kernels  140 us (90%)
  local copies, waits for them, and re-layouts  11.2 us (7%)
  other arithmetic  2.79 us (2%)
    pallas_call x1, Pallas kernels, call(): pl.pallas_call(functools.partial(kernel, n_dp, n_inv, cap), out_shape=jax...  140 us
    unnamed x4, local copies, waits for them, and re-layouts  10.2 us

profile of v2, /device:TPU:24, one launch (start us, length us, event | category | flops | bytes accessed | tf_op | source)
XLA Modules:
  0.0 154.3 jit_solution(9827985213487139005)
XLA Ops:
  0.0 1.3 reduce_sum.19
  1.9 0.8 select_reduce_fusion
  2.7 0.7 add_select_fusion
  3.4 0.0 copy-start
  3.4 1.9 %copy.8 = bf16[128,1536]{0,1:T(8,128)(2,1)} copy(bf16[128,1536]{1,0:T(8,128)(2,1)} %param.4) | data formatting | bytes 786432 | tf_op args[0]
  5.4 1.0 copy.9.pos_col
  6.4 0.0 copy-done
  6.4 139.6 %shard_map.46 = bf16[1536,3072]{1,0:T(8,128)(2,1)} custom-call(bf16[1536,128]{1,0:T(8,128)(2,1)} %bitcast.5, bf16[256,3072]{1,0:T(8,128)(2,1)} %grads.1, s32[1024,1]{1,0:T(8,128)} %copy.9.pos_col, s32[1,1024]{1,0:T(1,128)} %bitcast.7, s32[1,1024]{1,0:T(1,128)} %bitcast.8, f32[1,1]{1,0:T(1,128)} %bitcast.4.count), custom_call_target="tpu_custom_call" | custom-call | flops 21743271936 | bytes 18874368 | tf_op jit(solution)/shard_map/pallas_call | solution.py:363
  146.0 8.3 %copy.11 = bf16[1536,3072]{1,0:T(8,128)(2,1)} copy(bf16[1536,3072]{1,0:T(8,128)(2,1)} %shard_map.46) | data formatting | bytes 18874368
Async XLA Ops:
  3.4 2.9 %copy-start = (s32[8,128]{1,0:T(8,128)}, s32[8,128]{1,0:T(8,128)S(1)}, u32[]{:S(2)}) copy-start(s32[8,128]{1,0:T(8,128)S(1)} %add_select_fusion) | copy-start | bytes 12292

commit v3 on v2

--- a/solution.py
+++ b/solution.py
@@ -398,8 +398,15 @@
     pos = jnp.where(spot < shard_tokens[:, None], first[:, None] + spot, -1).astype(jnp.int32)
     count = jnp.sum(shard_tokens).astype(f32).reshape(1, 1)
     live = tokens * 3 // 4
-    return call(n_dp, n_inv, live, 0, acts.T, grads_out, pos.reshape(tokens, 1), pos.reshape(1, tokens),
-                scale_exp.reshape(1, tokens), count)
+    args = (acts.T, grads_out, pos.reshape(tokens, 1), pos.reshape(1, tokens), scale_exp.reshape(1, tokens), count)
+    full = functools.partial(call, n_dp, n_inv, live, 0)
+    tp = grads_out.shape[0]
+    cap = live * 5 // 6
+    if live - cap > tp:
+        return full(*args)
+    ends = shard_tokens.reshape(n_inv, tp // TOK_DEV).sum(axis=1)
+    few = jnp.minimum(ends[0], ends[-1]) >= live - cap
+    return lax.cond(few, functools.partial(call, n_dp, n_inv, cap, 1), full, *args)
 
 
 def solution(mesh):

time: 156 us -> 148 us (0.949)
  the two profiles are of different devices: /device:TPU:24 before, /device:TPU:8 now
where the time goes in v3:
time: 148 us
  Pallas kernels  130 us (88%)
  local copies, waits for them, and re-layouts  11.8 us (8%)
  other arithmetic  2.91 us (2%)
  between operations  2.02 us (1%)
    pallas_call x1, Pallas kernels, call(): pl.pallas_call(functools.partial(kernel, n_dp, n_inv, cap), out_shape=jax...  130 us
    unnamed x2, local copies, waits for them, and re-layouts  9.48 us

profile of v3, /device:TPU:8, one launch (start us, length us, event | category | flops | bytes accessed | tf_op | source)
XLA Modules:
  0.0 147.8 jit_solution(16701771596654429133)
XLA Ops:
  0.0 1.3 reduce_sum.29
  1.9 0.8 select_reduce_fusion
  2.7 0.7 reshape.117
  3.5 0.1 reduce_sum.27
  3.6 0.6 fusion
  5.5 0.7 add_select_fusion
  6.2 1.2 copy.17
  7.5 132.1 %conditional.1 = (bf16[1536,3072]{1,0:T(8,128)(2,1)}) conditional(s32[]{:T(128)} %bitcast.8, (bf16[1536,128]{1,0:T(8,128)(2,1)S(1)}, bf16[256,3072]{1,0:T(8,128)(2,1)}, s32[8,128]{1,0:T(8,128)S(1)}, s32[8,128]{1,0:T(8,128)S(1)}, s32[1024]{0:T(1024)}, /*index=5*/f32[]{:T(128)}) %tuple.17, (bf16[1536,128]{1,0:T(8,128)(2,1)S(1)}, ...), branch_computations={%region_3.4_spmd, %region_4.5_spmd} | conditional | flops 21743271936 | bytes 18882568 | solution.py:409
  7.7 1.0 copy.16.pos_col
  8.7 130.5 %branch_1_fun.1 = bf16[1536,3072]{1,0:T(8,128)(2,1)} custom-call(bf16[1536,128]{1,0:T(8,128)(2,1)S(1)} %get-tuple-element.38.acts_t, bf16[256,3072]{1,0:T(8,128)(2,1)} %get-tuple-element.56.grads, s32[1024,1]{1,0:T(8,128)} %copy.16.pos_col, s32[1,1024]{1,0:T(1,128)S(1)} %bitcast.15, s32[1,1024]{1,0:T(1,128)} %bitcast.17, f32[1,1]{1,0:T(1,128)} %bitcast.7.count), custom_call_target="tpu_custom_call" | custom-call | flops 21743271936 | bytes 18874368 | tf_op jit(solution)/shard_map/cond/branch_1_fun/pallas_call | solution.py:363
  139.5 8.3 %copy.21 = bf16[1536,3072]{1,0:T(8,128)(2,1)} copy(bf16[1536,3072]{1,0:T(8,128)(2,1)} %get-tuple-element.44) | data formatting | bytes 18874368
